TPU v7x, 32 devices: a whole 2x2x4 slice. The times are simulated.
32 devices in a mesh: lat: 4 (over x, core), lon: 8 (over z, y).
Axes of the slice: x: 2, y: 2, z: 4, core: 2. Of those that a mesh axis runs over, the one named last changes fastest.
Arguments:
- fields: bfloat16 [512, 1440, 256], P('lat', 'lon'), may hold values from -6 to 6
- basis: float32 [512, 4, 3, 17], P('lat'), may hold values from -1 to 1
- reach: int32 [512], P('lat'), may hold values from 1 to 8, as said below
- mixing: bfloat16 [4, 256, 256], replicated, may hold values from -0.1875 to 0.1875
- gains: float32 [2, 720, 256], replicated, may hold values from -5 to 5
Outputs:
- updated: bfloat16 [512, 1440, 256], P('lat', 'lon')
Inputs may be any that keep to these rules, and one draw needn't show every extreme that they name: `reach`: 8 is reached in some row.
All inputs are finite; a program needn't handle non-finite values.
Results may differ from a plain program's by a relative error of at most 0.0062.
Values may be sent and summed in bfloat16 or wider, within the bound.
A program may use at most 576 MiB of HBM per device.

v0:
```python
import jax
import jax.numpy as jnp
from jax import lax
from jax.sharding import PartitionSpec as P

NLON = 1440
MODES = 720
HALO = 8
WIN = 17


def with_halo(block, sides, width, periodic):
    for axis, dim in sides:
        count = lax.axis_size(axis)
        forward = [(i, i + 1) for i in range(count - 1)]
        if periodic:
            forward.append((count - 1, 0))
        backward = [(target, source) for source, target in forward]
        low = lax.ppermute(
            lax.slice_in_dim(block, block.shape[dim] - width, None, axis=dim), axis, forward
        )
        high = lax.ppermute(lax.slice_in_dim(block, 0, width, axis=dim), axis, backward)
        block = jnp.concatenate([low, block, high], axis=dim)
    return block


def make_tables(count, modes):
    index = jnp.arange(count, dtype=jnp.int32)
    wave = jnp.arange(modes, dtype=jnp.int32)
    phase = index[:, None] * wave[None, :] % count
    angle = phase.astype(jnp.float32) * (2.0 * jnp.pi / count)
    cosine = jnp.cos(angle)
    sine = jnp.sin(angle)
    forward = jnp.concatenate([cosine, -sine], 1)
    weights = jnp.where(wave == 0, 1.0, 2.0).astype(jnp.float32) / count
    weights = jnp.concatenate([weights, weights], 0)
    adjoint = forward * weights[None, :]
    return (forward.astype(jnp.bfloat16), adjoint.astype(jnp.bfloat16))


def transform(piece, forward, adjoint, gain_real, gain_imag):
    spectrum = jnp.einsum("rnc,nf->rfc", piece, forward, preferred_element_type=jnp.float32)
    real = spectrum[:, :MODES]
    imag = spectrum[:, MODES:]
    filtered = jnp.concatenate(
        [gain_real * real - gain_imag * imag, gain_real * imag + gain_imag * real], 1
    ).astype(jnp.bfloat16)
    return jnp.einsum("rfc,nf->rnc", filtered, adjoint, preferred_element_type=jnp.float32).astype(
        jnp.bfloat16
    )


def shards(fields, basis, reach, mixing, gains):
    lat_rows, lon_cols, chans = fields.shape
    wide = with_halo(fields, (("lon", 1),), HALO, True)
    padded = with_halo(wide, (("lat", 0),), 1, False)
    offsets = jnp.arange(WIN, dtype=jnp.int32) - HALO
    mask = (jnp.abs(offsets)[None, :] <= reach[:, None]).astype(jnp.float32)
    filters = (basis * mask[:, None, None, :]).astype(jnp.bfloat16)
    target = jnp.arange(lon_cols, dtype=jnp.int32)
    source = jnp.arange(lon_cols + 2 * HALO, dtype=jnp.int32)
    select = (
        source[None, :, None] - target[:, None, None] == offsets[None, None, :] + HALO
    ).astype(jnp.bfloat16)
    band = jnp.einsum(
        "ikab,jpb->ikjap", filters, select, preferred_element_type=jnp.float32
    ).astype(jnp.bfloat16)
    windows = jnp.stack([padded[0:lat_rows], padded[1 : lat_rows + 1], padded[2 : lat_rows + 2]], 1)
    conv = jnp.einsum("ikjap,iapc->ikjc", band, windows, preferred_element_type=jnp.float32).astype(
        jnp.bfloat16
    )
    local = jnp.einsum("ikjc,kcd->ijd", conv, mixing, preferred_element_type=jnp.float32)
    forward, adjoint = make_tables(NLON, MODES)
    gathered = lax.all_to_all(fields, "lon", split_axis=0, concat_axis=1, tiled=True)
    result = transform(gathered, forward, adjoint, gains[0], gains[1])
    back = lax.all_to_all(result, "lon", split_axis=1, concat_axis=0, tiled=True)
    return (fields.astype(jnp.float32) + local + back.astype(jnp.float32)).astype(jnp.bfloat16)


def solution(mesh):
    return jax.shard_map(
        shards,
        mesh=mesh,
        in_specs=(P("lat", "lon", None), P("lat", None, None, None), P("lat"), P(), P()),
        out_specs=P("lat", "lon", None),
        check_vma=False,
    )
```

profile of v0, /device:TPU:13, one launch (start us, length us, event | category | flops | bytes accessed | tf_op | source)
XLA Modules:
  0.0 1040.3 jit_solution(17651418187520683294)
XLA Ops:
  0.0 0.0 copy-start
  0.0 13.9 %copy.26 = bf16[128,180,256]{2,1,0:T(8,128)(2,1)} copy(bf16[128,180,256]{2,0,1:T(8,128)(2,1)} %param.5) | data formatting | bytes 23592960 | tf_op args[0]
  13.9 0.0 copy-start.1
  13.9 5.8 all-to-all-start
  19.7 0.1 pad_maximum_fusion.8
  19.7 0.0 copy-done.1
  19.7 1.0 slice_bitcast_fusion.1
  20.7 19.7 %sine_negate_fusion = (f32[1440,720]{0,1:T(8,128)}, f32[1440,720]{0,1:T(8,128)}) fusion(), kind=kLoop, calls=%fused_computation.40 | loop fusion | flops 10368000 | bytes 8294400 | tf_op jit(solution)/shard_map/neg | solution.py:34
  40.4 0.0 slice-start
  40.4 238.4 %all-to-all-done = bf16[128,180,256]{2,1,0:T(8,128)(2,1)} async-done(((bf16[128,180,256]{2,1,0:T(8,128)(2,1)}), bf16[128,180,256]{2,1,0:T(8,128)(2,1)}, u32[]{:S(2)}, u32[]{:S(2)}) %all-to-all-start) | async-done | bytes 11796512 | tf_op jit(solution)/shard_map/all_to_all | solution.py:74
  278.8 0.0 slice-start.1
  278.8 13.4 %copy.36 = bf16[16,8,180,256]{3,0,2,1:T(8,128)(2,1)S(1)} copy(bf16[16,8,180,256]{3,2,0,1:T(8,128)(2,1)} %bitcast.21) | data formatting | bytes 23592960 | tf_op jit(solution)/shard_map/all_to_all | solution.py:74
  292.2 0.0 slice-done
  292.2 0.0 slice-done.1
  292.2 27.4 %convolution_bitcast_fusion = f32[16,1440,256]{2,1,0:T(8,128)} fusion(bf16[16,1440,256]{2,0,1:T(8,128)(2,1)S(1)} %bitcast.85, f32[1440,720]{0,1:T(8,128)S(1)} %bitcast.87, f32[1440,720]{0,1:T(8,128)} %get-tuple-element.17), kind=kOutput, calls=%fused_computation.13 | convolution fusion | flops 16995225600 | bytes 43683840 | tf_op jit(solution)/shard_map/rnc,nf->rfc/dot_general | solution.py:42
  319.6 14.0 %subtract_convert_fusion = (bf16[16,720,256]{2,1,0:T(8,128)(2,1)}, bf16[16,720,256]{2,1,0:T(8,128)(2,1)}) fusion(f32[16,1440,256]{2,1,0:T(8,128)} %convolution_bitcast_fusion, f32[720,256]{1,0:T(8,128)} %get-tuple-element.15, f32[720,256]{1,0:T(8,128)S(1)} %get-tuple-element.14), kind=kLoop, calls=%fused_computation.29 | loop fusion | flops 23592960 | bytes 36864000 | tf_op jit(solution)/shard_map/convert.3
  333.6 24.8 %fusion.13 = bf16[16,1440,256]{2,1,0:T(8,128)(2,1)S(1)} fusion(bf16[16,720,256]{2,1,0:T(8,128)(2,1)} %get-tuple-element.6, bf16[16,720,256]{2,1,0:T(8,128)(2,1)} %get-tuple-element.5, f32[1440,720]{0,1:T(8,128)} %get-tuple-element.16, f32[1440,720]{0,1:T(8,128)} %get-tuple-element.17, f32[1440]{0:T(1024)S(1)} %pad_maximum_fusion.8), kind=kOutput, calls=%fused_computation.30 | convolution fusion | flops 17022643200 | bytes 31893120 | tf_op jit(solution)/shard_map/rfc,nf->rnc/dot_general | solution.py:48
  358.4 28.1 %copy.39 = bf16[16,1440,256]{2,0,1:T(8,128)(2,1)} copy(bf16[16,1440,256]{2,1,0:T(8,128)(2,1)S(1)} %fusion.13) | data formatting | bytes 23592960 | tf_op jit(solution)/shard_map/convert_element_type | solution.py:48
  386.5 0.0 copy-start.3
  386.5 0.0 copy-start.2
  386.5 7.1 all-to-all-start.1
  393.5 1.5 fusion.41
  395.0 0.3 collective-permute-start.1
  395.4 2.1 collective-permute-start
  397.5 0.0 copy-done.3
  397.5 0.1 compare_convert_fusion
  397.6 0.0 copy-done.2
  397.6 260.3 %collective-permute-done.1 = bf16[128,8,256]{2,1,0:T(8,128)(2,1)S(1)} collective-permute-done((bf16[128,8,256]{2,1,0:T(8,128)(2,1)S(1)}, bf16[128,8,256]{2,1,0:T(8,128)(2,1)S(1)}, u32[]{:S(2)}, u32[]{:S(2)}) %collective-permute-start.1) | collective-permute-done | bytes 524320 | tf_op jit(solution)/shard_map/ppermute | solution.py:22
  657.9 0.1 collective-permute-done
  658.1 7.1 pad_maximum_fusion.6
  665.2 5.6 collective-permute-start.2
  670.8 1.9 collective-permute-start.3
  672.7 39.5 %convert_bitcast_fusion = bf16[128,4,180,3,196]{0,4,3,1,2:T(8,128)(2,1)} fusion(s32[180,196]{1,0:T(8,128)S(1)} %iota_subtract_fusion, bf16[128,4,3,17]{0,1,3,2:T(4,128)(2,1)S(1)} %multiply_convert_fusion.1), kind=kOutput, calls=%fused_computation | convolution fusion | flops 1897252608 | bytes 108573504 | tf_op jit(solution)/shard_map/ikab,jpb->ikjap/dot_general | solution.py:65
  712.2 174.6 %copy.33 = bf16[128,4,180,3,196]{4,2,3,1,0:T(8,128)(2,1)} copy(bf16[128,4,180,3,196]{0,4,3,1,2:T(8,128)(2,1)} %convert_bitcast_fusion) | data formatting | bytes 216760320 | tf_op jit(solution)/shard_map/convert_element_type | solution.py:67
  886.8 0.0 collective-permute-done.2
  886.8 0.0 collective-permute-done.3
  886.8 32.2 %fusion.8 = (bf16[128,1,196,256]{3,2,1,0:T(8,128)(2,1)}, bf16[128,1,196,256]{3,2,1,0:T(8,128)(2,1)}, bf16[128,1,196,256]{3,2,1,0:T(8,128)(2,1)}) fusion(bf16[1,196,256]{2,1,0:T(8,128)(2,1)S(1)} %collective-permute-done.2, bf16[128,8,256]{2,1,0:T(8,128)(2,1)S(1)} %collective-permute-done.1, bf16[128,180,256]{2,1,0:T(8,128)(2,1)} %copy.26, ...), kind=kLoop, calls=%fused_computation.20 | loop fusion | flops 141295616 | bytes 51580928 | tf_op jit(solution)/shard_map/stack | solution.py:68
  919.0 0.0 all-to-all-done.1
  919.0 7.1 convert_bitcast_fusion.1
  926.2 16.6 %copy.40 = f32[8,16,180,256]{3,2,1,0:T(8,128)} copy(f32[8,16,180,256]{3,1,2,0:T(8,128)S(1)} %convert_bitcast_fusion.1) | data formatting | bytes 47185920 | tf_op jit(solution)/shard_map/convert_element_type | solution.py:77
  942.8 0.0 copy-done
  942.8 81.1 %fusion.6 = bf16[128,180,256]{2,1,0:T(8,128)(2,1)} fusion(f32[8,16,180,256]{3,2,1,0:T(8,128)} %copy.40, bf16[128,4,180,3,196]{4,2,3,1,0:T(8,128)(2,1)} %copy.33, bf16[128,1,196,256]{3,2,1,0:T(8,128)(2,1)} %get-tuple-element.9, bf16[128,1,196,256]{3,2,1,0:T(8,128)(2,1)} %get-tuple-element.8, bf16[128,1,196,256]{3,2,1,0:T(8,128)(2,1)} %get-tuple-element.7, ...), kind=kOutput, calls=%fused_computation.10 | convolution fusion | flops 39910637568 | bytes 194625536 | tf_op jit(solution)/shard_map/ikjc,kcd->ijd/dot_general | solution.py:72
  1023.9 16.1 %copy.41 = bf16[128,180,256]{2,0,1:T(8,128)(2,1)} copy(bf16[128,180,256]{2,1,0:T(8,128)(2,1)} %fusion.6) | data formatting | bytes 23592960 | tf_op jit(solution)/shard_map/convert_element_type | solution.py:77
  (6 shorter events, 0.1 us)
Async XLA Ops:
  0.0 942.8 %copy-start = (bf16[4,256,256]{2,1,0:T(8,128)(2,1)S(1)}, bf16[4,256,256]{2,1,0:T(8,128)(2,1)}, u32[]{:S(2)}) copy-start(bf16[4,256,256]{2,1,0:T(8,128)(2,1)} %param.8) | copy-start | bytes 1572868
  13.9 5.9 copy-start.1
  13.9 265.0 %all-to-all-start = ((bf16[128,180,256]{2,1,0:T(8,128)(2,1)}), bf16[128,180,256]{2,1,0:T(8,128)(2,1)}, u32[]{:S(2)}, u32[]{:S(2)}) async-start(bf16[128,180,256]{2,1,0:T(8,128)(2,1)} %copy.26), calls=%async_computation | async-start | bytes 24117248 | tf_op jit(solution)/shard_map/all_to_all | solution.py:74
  40.4 251.8 %slice-start = ((s8[4423680]{0:T(1024)(128)(4,1)}), s8[229376]{0:T(1024)(128)(4,1)S(1)}, s32[]{:S(2)}) async-start(s8[4423680]{0:T(1024)(128)(4,1)} %bitcast.86), calls=%async_computation.2 | async-start | bytes 458752
  278.8 13.4 %slice-start.1 = ((s8[4423680]{0:T(1024)(128)(4,1)}), s8[4194304]{0:T(1024)(128)(4,1)S(1)}, s32[]{:S(2)}) async-start(s8[4423680]{0:T(1024)(128)(4,1)} %bitcast.86), calls=%async_computation.3 | async-start | bytes 8388608
  386.5 11.0 %copy-start.3 = (s32[128]{0:T(128)S(1)}, s32[128]{0:T(128)}, u32[]{:S(2)}) copy-start(s32[128]{0:T(128)} %param.7) | copy-start | bytes 1540
  386.5 11.1 %copy-start.2 = (f32[128,4,3,17]{0,1,3,2:T(4,128)S(1)}, f32[128,4,3,17]{0,1,3,2:T(4,128)}, u32[]{:S(2)}) copy-start(f32[128,4,3,17]{0,1,3,2:T(4,128)} %param.6) | copy-start | bytes 313348
  386.5 532.6 %all-to-all-start.1 = ((bf16[16,1440,256]{2,0,1:T(8,128)(2,1)}), bf16[16,1440,256]{2,0,1:T(8,128)(2,1)}, u32[]{:S(2)}, u32[]{:S(2)}) async-start(bf16[16,1440,256]{2,0,1:T(8,128)(2,1)} %copy.39), calls=%async_computation.1 | async-start | bytes 23592960 | tf_op jit(solution)/shard_map/all_to_all | solution.py:76
  395.0 262.9 %collective-permute-start.1 = (bf16[128,8,256]{2,1,0:T(8,128)(2,1)S(1)}, bf16[128,8,256]{2,1,0:T(8,128)(2,1)S(1)}, u32[]{:S(2)}, u32[]{:S(2)}) collective-permute-start(bf16[128,8,256]{2,1,0:T(8,128)(2,1)S(1)} %get-tuple-element.13), channel_id=1, source_target_pairs={{1,0},{2,1},{3,2},{4,3},{5,4},{6,5},{7,6},{0,7},{9,8},{10,9},{11,1... | collective-permute-start | bytes 1572872 | tf_op jit(solution)/shard_map/ppermute | solution.py:22
  395.4 262.7 %collective-permute-start = (bf16[128,8,256]{2,1,0:T(8,128)(2,1)S(1)}, bf16[128,8,256]{2,1,0:T(8,128)(2,1)S(1)}, u32[]{:S(2)}, u32[]{:S(2)}) collective-permute-start(bf16[128,8,256]{2,1,0:T(8,128)(2,1)S(1)} %get-tuple-element.12), channel_id=1, source_target_pairs={{0,1},{1,2},{2,3},{3,4},{4,5},{5,6},{6,7},{7,0},{8,9},{9,10},{10,1... | collective-permute-start | bytes 1572872 | tf_op jit(solution)/shard_map/ppermute | solution.py:19
  665.2 221.6 %collective-permute-start.2 = (bf16[1,196,256]{2,1,0:T(8,128)(2,1)S(1)}, bf16[1,196,256]{2,1,0:T(8,128)(2,1)S(1)}, u32[]{:S(2)}, u32[]{:S(2)}) collective-permute-start(bf16[1,196,256]{2,1,0:T(8,128)(2,1)S(1)} %get-tuple-element.10), channel_id=1, source_target_pairs={{0,8},{8,16},{16,24},{1,9},{9,17},{17,25},{2,10},{10,18},{18,26},{... | collective-permute-start | bytes 301064 | tf_op jit(solution)/shard_map/ppermute | solution.py:19
  670.8 216.1 %collective-permute-start.3 = (bf16[1,196,256]{2,1,0:T(8,128)(2,1)S(1)}, bf16[1,196,256]{2,1,0:T(8,128)(2,1)S(1)}, u32[]{:S(2)}, u32[]{:S(2)}) collective-permute-start(bf16[1,196,256]{2,1,0:T(8,128)(2,1)S(1)} %get-tuple-element.11), channel_id=1, source_target_pairs={{8,0},{16,8},{24,16},{9,1},{17,9},{25,17},{10,2},{18,10},{26,18},{... | collective-permute-start | bytes 301064 | tf_op jit(solution)/shard_map/ppermute | solution.py:22
where the time goes:
time: 1050 us; the launch traced here: 1040 us
  waiting for transfers between devices  499 us (48%)
  local copies, waits for them, and re-layouts  265 us (25%)
  matrix products  173 us (16%)
  other arithmetic  80.3 us (8%)
  starting transfers between devices  22.8 us (2%)
    ppermute x2, waiting for transfers between devices, with_halo(): lax.ppermute(lax.slice_in_dim(block, 0, width, axis=dim), axis, backward)  260 us
    all_to_all x1, waiting for transfers between devices, shards(): lax.all_to_all(fields, 'lon', split_axis=0, concat_axis=1, tiled=True)  238 us
    convert_element_type x1, local copies, waits for them, and re-layouts, shards(): band = jnp.einsum('ikab,jpb->ikjap', filters, select, preferred_element_t...  175 us
    dot_general x1, matrix products, shards(): jnp.einsum('ikjc,kcd->ijd', conv, mixing, preferred_element_type=jnp.floa...  81.1 us
    dot_general x1, matrix products, shards(): jnp.einsum('ikab,jpb->ikjap', filters, select, preferred_element_type=jnp...  39.5 us
    another operation x1, other arithmetic, shards(): jnp.stack([padded[0:lat_rows], padded[1:lat_rows + 1], padded[2:lat_rows...  32.2 us
    convert_element_type x1, local copies, waits for them, and re-layouts, transform(): jnp.einsum('rfc,nf->rnc', filtered, adjoint, preferred_element_type=jnp.f...  28.1 us
    dot_general x1, matrix products, transform(): jnp.einsum('rnc,nf->rfc', piece, forward, preferred_element_type=jnp.floa...  27.4 us
  transfers between devices with their start and end apart: 6, of which 3 were waited for; matrix products, arithmetic and copies ran while one was open for 27% of the time, Pallas kernels for 0%

commit v1 on v0

--- a/solution.py
+++ b/solution.py
@@ -1,3 +1,4 @@
+import functools
 import jax
 import jax.numpy as jnp
 from jax import lax
@@ -7,6 +8,19 @@
 MODES = 720
 HALO = 8
 WIN = 17
+
+
+def advance_rows_on_mesh(vals, axis_k, dim_k):
+    local_out = jnp.concatenate(
+        lax.all_to_all(
+            jnp.stack(jnp.split(vals, lax.axis_size("lon"), axis=axis_k), axis=0), "lon", 0, 0
+        ),
+        axis=dim_k,
+    )
+    return local_out
+
+
+rest_the_leaves = functools.partial(advance_rows_on_mesh, axis_k=0, dim_k=1)
 
 
 def with_halo(block, sides, width, periodic):
@@ -71,7 +85,7 @@
     )
     local = jnp.einsum("ikjc,kcd->ijd", conv, mixing, preferred_element_type=jnp.float32)
     forward, adjoint = make_tables(NLON, MODES)
-    gathered = lax.all_to_all(fields, "lon", split_axis=0, concat_axis=1, tiled=True)
+    gathered = rest_the_leaves(fields)
     result = transform(gathered, forward, adjoint, gains[0], gains[1])
     back = lax.all_to_all(result, "lon", split_axis=1, concat_axis=0, tiled=True)
     return (fields.astype(jnp.float32) + local + back.astype(jnp.float32)).astype(jnp.bfloat16)

time: 1050 us -> 788 us (0.75)
  waiting for transfers between devices: 499 us -> 231 us
  other arithmetic: 80.3 us -> 109 us
  local copies, waits for them, and re-layouts: 265 us -> 254 us
    all_to_all x1, waiting for transfers between devices: 238 us -> 0.01 us  [advance_rows_on_mesh(): lax.all_to_all(jnp.stack(jnp.split(vals, lax.axis_size('lon'), axis=axis_...]
    ppermute x2, waiting for transfers between devices: 260 us -> 231 us  [with_halo(): lax.ppermute(lax.slice_in_dim(block, 0, width, axis=dim), axis, backward)]
    convert_element_type x0 -> x1, other arithmetic: none -> 23.4 us  [shards(): (fields.astype(jnp.float32) + local + back.astype(jnp.float32)).astype(jn...]
    unnamed x13 -> x34, local copies, waits for them, and re-layouts: 13.9 us -> 30.4 us
    convert_element_type x1 -> x0, local copies, waits for them, and re-layouts: 16.1 us -> none  [shards(): (fields.astype(jnp.float32) + local + back.astype(jnp.float32)).astype(jn...]
    all_to_all x1 -> x0, local copies, waits for them, and re-layouts: 13.4 us -> none  [shards(): lax.all_to_all(fields, 'lon', split_axis=0, concat_axis=1, tiled=True)]
  transfers between devices with their start and end apart: 6 -> 6, of which waited for: 3 -> 1; matrix products, arithmetic and copies ran while one was open for 27% -> 58% of each run, Pallas kernels for 0% -> 0%
where the time goes in v1:
time: 788 us; the launch traced here: 779 us
  local copies, waits for them, and re-layouts  254 us (32%)
  waiting for transfers between devices  231 us (29%)
  matrix products  164 us (21%)
  other arithmetic  109 us (14%)
  starting transfers between devices  20.5 us (3%)
    ppermute x2, waiting for transfers between devices, with_halo(): lax.ppermute(lax.slice_in_dim(block, 0, width, axis=dim), axis, backward)  231 us
    convert_element_type x1, local copies, waits for them, and re-layouts, shards(): band = jnp.einsum('ikab,jpb->ikjap', filters, select, preferred_element_t...  175 us
    dot_general x1, matrix products, shards(): jnp.einsum('ikjc,kcd->ijd', conv, mixing, preferred_element_type=jnp.floa...  74.3 us
    dot_general x1, matrix products, shards(): jnp.einsum('ikab,jpb->ikjap', filters, select, preferred_element_type=jnp...  39.4 us
    another operation x1, other arithmetic, shards(): jnp.stack([padded[0:lat_rows], padded[1:lat_rows + 1], padded[2:lat_rows...  32.4 us
    unnamed x34, local copies, waits for them, and re-layouts  30.4 us
    convert_element_type x1, local copies, waits for them, and re-layouts, transform(): jnp.einsum('rfc,nf->rnc', filtered, adjoint, preferred_element_type=jnp.f...  28.2 us
    dot_general x1, matrix products, transform(): jnp.einsum('rnc,nf->rfc', piece, forward, preferred_element_type=jnp.floa...  26.3 us
  transfers between devices with their start and end apart: 6, of which 1 were waited for; matrix products, arithmetic and copies ran while one was open for 58% of the time, Pallas kernels for 0%

profile of v1, /device:TPU:13, one launch (start us, length us, event | category | flops | bytes accessed | tf_op | source)
XLA Modules:
  0.0 778.6 jit_solution(4508286108227091206)
XLA Ops:
  0.0 0.0 copy-start
  0.0 2.7 bitcast_dynamic-update-slice_fusion.7
  2.7 2.6 bitcast_dynamic-update-slice_fusion.6
  5.3 2.6 bitcast_dynamic-update-slice_fusion.5
  7.9 2.6 bitcast_dynamic-update-slice_fusion.4
  10.5 2.6 bitcast_dynamic-update-slice_fusion.3
  13.1 2.6 bitcast_dynamic-update-slice_fusion.2
  15.7 2.6 bitcast_dynamic-update-slice_fusion.1
  18.3 2.6 bitcast_dynamic-update-slice_fusion
  20.9 5.7 all-to-all-start
  26.5 12.1 %copy.14 = bf16[128,180,256]{2,1,0:T(8,128)(2,1)S(1)} copy(bf16[128,180,256]{2,0,1:T(8,128)(2,1)} %param.5) | data formatting | bytes 23592960 | tf_op args[0]
  38.6 0.0 copy-start.2
  38.6 0.2 fusion.41
  38.8 0.3 collective-permute-start.1
  39.2 2.1 collective-permute-start
  41.3 0.0 copy-done.9
  41.3 0.1 compare_convert_fusion
  41.3 0.0 copy-done.8
  41.4 0.1 slice_bitcast_fusion.1
  41.5 0.1 pad_maximum_fusion.8
  41.6 19.7 %sine_negate_fusion = (f32[1440,720]{0,1:T(8,128)}, f32[1440,720]{0,1:T(8,128)}) fusion(), kind=kLoop, calls=%fused_computation.40 | loop fusion | flops 10368000 | bytes 8294400 | tf_op jit(solution)/shard_map/neg | solution.py:48
  61.3 230.5 %collective-permute-done.1 = bf16[128,8,256]{2,1,0:T(8,128)(2,1)S(1)} collective-permute-done((bf16[128,8,256]{2,1,0:T(8,128)(2,1)S(1)}, bf16[128,8,256]{2,1,0:T(8,128)(2,1)S(1)}, u32[]{:S(2)}, u32[]{:S(2)}) %collective-permute-start.1) | collective-permute-done | bytes 524320 | tf_op jit(solution)/shard_map/ppermute | solution.py:36
  291.8 0.0 collective-permute-done
  291.8 3.0 pad_maximum_fusion.6
  294.8 0.7 fusion.40
  295.5 4.8 collective-permute-start.2
  300.3 2.4 collective-permute-start.3
  302.7 0.0 all-to-all-done
  302.8 26.3 %convolution_bitcast_fusion = f32[16,1440,256]{2,1,0:T(8,128)} fusion(bf16[16,1440,256]{2,0,1:T(8,128)(2,1)} %bitcast.27, f32[1440,720]{0,1:T(8,128)} %get-tuple-element.16, f32[1440,720]{0,1:T(8,128)} %get-tuple-element.17), kind=kOutput, calls=%fused_computation.13 | convolution fusion | flops 16995225600 | bytes 43683840 | tf_op jit(solution)/shard_map/rnc,nf->rfc/dot_general | solution.py:56
  329.0 13.8 %subtract_convert_fusion = (bf16[16,720,256]{2,1,0:T(8,128)(2,1)}, bf16[16,720,256]{2,1,0:T(8,128)(2,1)}) fusion(f32[16,1440,256]{2,1,0:T(8,128)} %convolution_bitcast_fusion, f32[720,256]{1,0:T(8,128)S(1)} %get-tuple-element.15, f32[720,256]{1,0:T(8,128)S(1)} %get-tuple-element.14), kind=kLoop, calls=%fused_computation.29 | loop fusion | flops 23592960 | bytes 36864000 | tf_op jit(solution)/shard_map/convert.3
  342.8 24.3 %fusion.13 = bf16[16,1440,256]{2,1,0:T(8,128)(2,1)S(1)} fusion(bf16[16,720,256]{2,1,0:T(8,128)(2,1)} %get-tuple-element.6, bf16[16,720,256]{2,1,0:T(8,128)(2,1)} %get-tuple-element.5, f32[1440,720]{0,1:T(8,128)} %get-tuple-element.16, f32[1440,720]{0,1:T(8,128)} %get-tuple-element.17, f32[1440]{0:T(1024)S(1)} %pad_maximum_fusion.8), kind=kOutput, calls=%fused_computation.30 | convolution fusion | flops 17022643200 | bytes 31893120 | tf_op jit(solution)/shard_map/rfc,nf->rnc/dot_general | solution.py:62
  367.2 28.2 %copy.23 = bf16[16,1440,256]{2,0,1:T(8,128)(2,1)} copy(bf16[16,1440,256]{2,1,0:T(8,128)(2,1)S(1)} %fusion.13) | data formatting | bytes 23592960 | tf_op jit(solution)/shard_map/convert_element_type | solution.py:62
  395.4 5.2 all-to-all-start.1
  400.6 39.4 %convert_bitcast_fusion = bf16[128,4,180,3,196]{0,4,3,1,2:T(8,128)(2,1)} fusion(s32[180,196]{1,0:T(8,128)S(1)} %iota_subtract_fusion, bf16[128,4,3,17]{0,1,3,2:T(4,128)(2,1)S(1)} %multiply_convert_fusion.1), kind=kOutput, calls=%fused_computation | convolution fusion | flops 1897252608 | bytes 108573504 | tf_op jit(solution)/shard_map/ikab,jpb->ikjap/dot_general | solution.py:79
  440.0 174.6 %copy.19 = bf16[128,4,180,3,196]{4,2,3,1,0:T(8,128)(2,1)} copy(bf16[128,4,180,3,196]{0,4,3,1,2:T(8,128)(2,1)} %convert_bitcast_fusion) | data formatting | bytes 216760320 | tf_op jit(solution)/shard_map/convert_element_type | solution.py:81
  614.6 0.0 collective-permute-done.2
  614.6 0.0 collective-permute-done.3
  614.6 0.0 copy-done.4
  614.6 0.0 copy-done.6
  614.6 32.4 %fusion.8 = (bf16[128,1,196,256]{3,2,1,0:T(8,128)(2,1)}, bf16[128,1,196,256]{3,2,1,0:T(8,128)(2,1)}, bf16[128,1,196,256]{3,2,1,0:T(8,128)(2,1)}) fusion(bf16[1,196,256]{2,1,0:T(8,128)(2,1)} %collective-permute-done.2, bf16[128,8,256]{2,1,0:T(8,128)(2,1)S(1)} %copy-done.4, bf16[128,180,256]{2,1,0:T(8,128)(2,1)} %copy-done.2, ...), kind=kLoop, calls=%fused_computation.20 | loop fusion | flops 141295616 | bytes 51580928 | tf_op jit(solution)/shard_map/stack | solution.py:82
  647.0 74.3 %fusion = f32[128,180,256,1]{2,1,3,0:T(8,128)} fusion(bf16[128,4,180,3,196]{4,2,3,1,0:T(8,128)(2,1)} %copy.19, bf16[128,1,196,256]{3,2,1,0:T(8,128)(2,1)} %get-tuple-element.9, bf16[128,1,196,256]{3,2,1,0:T(8,128)(2,1)} %get-tuple-element.8, bf16[128,1,196,256]{3,2,1,0:T(8,128)(2,1)} %get-tuple-element.7, bf16[4,256,256]{2,1,0:T(8,128)(2,1)S(1)} %copy-done), kind=kOutput, calls=%fused_computation.2 | convolution fusion | flops 39887044608 | bytes 171032576 | tf_op jit(solution)/shard_map/ikjc,kcd->ijd/dot_general | solution.py:86
  721.3 0.0 all-to-all-done.1
  721.3 0.0 slice-start.1
  721.3 16.3 %convert_bitcast_fusion.1 = f32[8,16,180,256]{3,1,2,0:T(8,128)} fusion(bf16[16,8,180,256]{3,0,2,1:T(8,128)(2,1)} %bitcast.39), kind=kLoop, calls=%fused_computation.9 | loop fusion | flops 5898240 | bytes 35389440 | tf_op jit(solution)/shard_map/convert_element_type | solution.py:91
  737.6 17.4 %copy.24 = f32[8,16,180,256]{3,1,0,2:T(8,128)} copy(f32[8,16,180,256]{3,1,2,0:T(8,128)} %convert_bitcast_fusion.1) | data formatting | bytes 47185920 | tf_op jit(solution)/shard_map/convert_element_type | solution.py:91
  755.0 0.0 slice-done.1
  755.0 0.0 copy-start.1
  755.0 23.4 %fusion.6 = bf16[128,180,256]{2,0,1:T(8,128)(2,1)} fusion(f32[8,16,180,256]{3,1,0,2:T(8,128)} %copy.24, f32[128,180,256,1]{2,1,3,0:T(8,128)} %fusion, bf16[128,180,256]{2,0,1:T(8,128)(2,1)S(1)} %bitcast.94), kind=kLoop, calls=%fused_computation.11 | loop fusion | flops 23592960 | bytes 70778880 | tf_op jit(solution)/shard_map/convert_element_type | solution.py:91
  (22 shorter events, 0.1 us)
Async XLA Ops:
  0.0 647.0 %copy-start = (bf16[4,256,256]{2,1,0:T(8,128)(2,1)S(1)}, bf16[4,256,256]{2,1,0:T(8,128)(2,1)}, u32[]{:S(2)}) copy-start(bf16[4,256,256]{2,1,0:T(8,128)(2,1)} %param.8) | copy-start | bytes 1572868
  20.9 281.9 %all-to-all-start = ((bf16[8,16,180,256]{3,1,2,0:T(8,128)(2,1)}), bf16[8,16,180,256]{3,1,2,0:T(8,128)(2,1)}, u32[]{:S(2)}, u32[]{:S(2)}) async-start(bf16[8,16,180,256]{3,1,2,0:T(8,128)(2,1)} %bitcast_dynamic-update-slice_fusion), calls=%async_computation | async-start | bytes 23592960 | tf_op jit(solution)/shard_map/all_to_all | solution.py:15
  26.5 14.7 %copy-start.9 = (s32[128]{0:T(128)S(1)}, s32[128]{0:T(128)}, u32[]{:S(2)}) copy-start(s32[128]{0:T(128)} %param.7) | copy-start | bytes 1540
  26.5 14.8 %copy-start.8 = (f32[128,4,3,17]{0,1,3,2:T(4,128)S(1)}, f32[128,4,3,17]{0,1,3,2:T(4,128)}, u32[]{:S(2)}) copy-start(f32[128,4,3,17]{0,1,3,2:T(4,128)} %param.6) | copy-start | bytes 313348
  26.5 14.8 %copy-start.7 = (f32[2,720,256]{2,1,0:T(8,128)S(1)}, f32[2,720,256]{2,1,0:T(8,128)}, u32[]{:S(2)}) copy-start(f32[2,720,256]{2,1,0:T(8,128)} %param.9) | copy-start | bytes 4423684
  38.6 256.2 %copy-start.2 = (bf16[128,180,256]{2,1,0:T(8,128)(2,1)}, bf16[128,180,256]{2,1,0:T(8,128)(2,1)S(1)}, u32[]{:S(2)}) copy-start(bf16[128,180,256]{2,1,0:T(8,128)(2,1)S(1)} %copy.14) | copy-start | bytes 35389444
  38.8 253.0 %collective-permute-start.1 = (bf16[128,8,256]{2,1,0:T(8,128)(2,1)S(1)}, bf16[128,8,256]{2,1,0:T(8,128)(2,1)S(1)}, u32[]{:S(2)}, u32[]{:S(2)}) collective-permute-start(bf16[128,8,256]{2,1,0:T(8,128)(2,1)S(1)} %get-tuple-element.13), channel_id=1, source_target_pairs={{1,0},{2,1},{3,2},{4,3},{5,4},{6,5},{7,6},{0,7},{9,8},{10,9},{11,1... | collective-permute-start | bytes 1572872 | tf_op jit(solution)/shard_map/ppermute | solution.py:36
  39.2 252.7 %collective-permute-start = (bf16[128,8,256]{2,1,0:T(8,128)(2,1)S(1)}, bf16[128,8,256]{2,1,0:T(8,128)(2,1)S(1)}, u32[]{:S(2)}, u32[]{:S(2)}) collective-permute-start(bf16[128,8,256]{2,1,0:T(8,128)(2,1)S(1)} %get-tuple-element.12), channel_id=1, source_target_pairs={{0,1},{1,2},{2,3},{3,4},{4,5},{5,6},{6,7},{7,0},{8,9},{9,10},{10,1... | collective-permute-start | bytes 1572872 | tf_op jit(solution)/shard_map/ppermute | solution.py:33
  291.8 3.0 copy-start.3
  291.8 3.0 copy-start.5
  295.5 319.1 %collective-permute-start.2 = (bf16[1,196,256]{2,1,0:T(8,128)(2,1)}, bf16[1,196,256]{2,1,0:T(8,128)(2,1)}, u32[]{:S(2)}, u32[]{:S(2)}) collective-permute-start(bf16[1,196,256]{2,1,0:T(8,128)(2,1)} %get-tuple-element.10), channel_id=1, source_target_pairs={{0,8},{8,16},{16,24},{1,9},{9,17},{17,25},{2,10},{10,18},{18,26},{... | collective-permute-start | bytes 301064 | tf_op jit(solution)/shard_map/ppermute | solution.py:33
  300.3 314.2 %collective-permute-start.3 = (bf16[1,196,256]{2,1,0:T(8,128)(2,1)}, bf16[1,196,256]{2,1,0:T(8,128)(2,1)}, u32[]{:S(2)}, u32[]{:S(2)}) collective-permute-start(bf16[1,196,256]{2,1,0:T(8,128)(2,1)} %get-tuple-element.11), channel_id=1, source_target_pairs={{8,0},{16,8},{24,16},{9,1},{17,9},{25,17},{10,2},{18,10},{26,18},{... | collective-permute-start | bytes 301064 | tf_op jit(solution)/shard_map/ppermute | solution.py:36
  395.4 325.9 %all-to-all-start.1 = ((bf16[16,1440,256]{2,0,1:T(8,128)(2,1)}), bf16[16,1440,256]{2,0,1:T(8,128)(2,1)}, u32[]{:S(2)}, u32[]{:S(2)}) async-start(bf16[16,1440,256]{2,0,1:T(8,128)(2,1)} %copy.23), calls=%async_computation.1 | async-start | bytes 23592960 | tf_op jit(solution)/shard_map/all_to_all | solution.py:90
  440.0 174.6 %copy-start.4 = (bf16[128,8,256]{2,1,0:T(8,128)(2,1)S(1)}, bf16[128,8,256]{2,1,0:T(8,128)(2,1)}, u32[]{:S(2)}) copy-start(bf16[128,8,256]{2,1,0:T(8,128)(2,1)} %copy-done.3) | copy-start | bytes 1572868
  440.0 174.6 %copy-start.6 = (bf16[128,8,256]{2,1,0:T(8,128)(2,1)S(1)}, bf16[128,8,256]{2,1,0:T(8,128)(2,1)}, u32[]{:S(2)}) copy-start(bf16[128,8,256]{2,1,0:T(8,128)(2,1)} %copy-done.5) | copy-start | bytes 1572868
  721.3 33.7 %slice-start = ((s8[11796480]{0:T(1024)(128)(4,1)}), s8[4194304]{0:T(1024)(128)(4,1)S(1)}, s32[]{:S(2)}) async-start(s8[11796480]{0:T(1024)(128)(4,1)} %bitcast.93), calls=%async_computation.2 | async-start | bytes 8388608
  721.3 33.7 %slice-start.1 = ((s8[11796480]{0:T(1024)(128)(4,1)}), s8[4194304]{0:T(1024)(128)(4,1)S(1)}, s32[]{:S(2)}) async-start(s8[11796480]{0:T(1024)(128)(4,1)} %bitcast.93), calls=%async_computation.3 | async-start | bytes 8388608
  737.6 17.4 %slice-start.2 = ((s8[11796480]{0:T(1024)(128)(4,1)}), s8[3407872]{0:T(1024)(128)(4,1)S(1)}, s32[]{:S(2)}) async-start(s8[11796480]{0:T(1024)(128)(4,1)} %bitcast.93), calls=%async_computation.4 | async-start | bytes 6815744
  755.0 23.4 %copy-start.1 = (bf16[4,256,256]{2,1,0:T(8,128)(2,1)S(1)}, bf16[4,256,256]{2,1,0:T(8,128)(2,1)}, u32[]{:S(2)}) copy-start(bf16[4,256,256]{2,1,0:T(8,128)(2,1)} %param.8) | copy-start | bytes 1572868
